TPU v7x, 32 devices: a whole 2x2x4 slice. The times are simulated.
32 devices in a mesh: row: 4 (over z), col: 8 (over y, x, core).
Axes of the slice: x: 2, y: 2, z: 4, core: 2. Of those that a mesh axis runs over, the one named last changes fastest.
Arguments:
- offsets: float32 [4, 8, 2, 256], P('row', 'col'), may hold values from 0 to 1
- point_order: int32 [4, 8, 256], P('row', 'col'), may hold values from 0 to 255, each once within a row
- nugget: float32 [4, 8, 256], P('row', 'col'), may hold values from 1 to 4
- interp: float32 [4, 8, 128, 128], P('row', 'col'), may hold values from -0.5 to 0.5
Outputs:
- root_work: float32 [4096, 4096], P('row', 'col')
Inputs may be any that keep to these rules, and one draw needn't show every extreme that they name: `point_order`: each row lists every point of its box once; its first 128 entries name the box's skeleton points.
All inputs are finite; a program needn't handle non-finite values.
Results may differ from a plain program's by a relative error of at most 0.0001.
Values sent between devices are 32-bit elements; how exact they have to be, the bound alone decides.
No kernel may reach another device: no remote copies, remote signals or barrier semaphores. Data moves between devices by JAX's collectives and lax.ppermute only.
A program may use at most 128 MiB of HBM per device.

v0:
```python
import jax
import jax.numpy as jnp
from jax import lax
from jax.sharding import PartitionSpec as P

PW = 512


kernel_amp = 0.015625
kernel_len = 0.5
highest = lax.Precision.HIGHEST


def extended(block, sides, width):
    for axis, dim in sides:
        count = lax.axis_size(axis)
        forward = [(i, i + 1) for i in range(count - 1)]
        backward = [(target, source) for source, target in forward]
        low = lax.ppermute(
            lax.slice_in_dim(block, block.shape[dim] - width, None, axis=dim), axis, forward
        )
        high = lax.ppermute(lax.slice_in_dim(block, 0, width, axis=dim), axis, backward)
        block = jnp.concatenate([low, block, high], axis=dim)
    return block


def shifted(block, axis, distance):
    devices = range(lax.axis_size(axis))
    route = [(i - distance, i) for i in devices if i - distance in devices]
    return lax.ppermute(block, axis, route)


def spread_2(value, axis, source):
    kept = jnp.where(lax.axis_index(axis) == source, value, 0).astype(value.dtype)
    return lax.psum(kept, axis)


def offsets_all():
    return [(a, b) for a in (-1, 0, 1) for b in (-1, 0, 1)]


def pairs_all():
    return [
        (e, m)
        for e in offsets_all()
        for m in offsets_all()
        if abs(m[0] - e[0]) <= 1 and abs(m[1] - e[1]) <= 1
    ]


def block_of(a, b):
    return (a + 1) * 3 + (b + 1)


def vector(along, across):
    return (along, across)


def kernel(left, right):
    gap_row = left[0][:, None] - right[0][None, :]
    gap_col = left[1][:, None] - right[1][None, :]
    return kernel_amp * jnp.exp(-jnp.sqrt(gap_row * gap_row + gap_col * gap_col) / kernel_len)


def cross_pair(stored, target, columns):
    pair_index = {pair: n for n, pair in enumerate(pairs_all())}
    left_rows = []
    right_rows = []
    for e in offsets_all():
        if abs(target[0] - e[0]) <= 1 and abs(target[1] - e[1]) <= 1:
            left_rows.append(stored[pair_index[e, (0, 0)]][:, :columns])
            right_rows.append(stored[pair_index[e, target]][:, :columns])
    return (jnp.concatenate(left_rows, axis=0), jnp.concatenate(right_rows, axis=0))


def cross_sum(stored, target, columns):
    left_rows, right_rows = cross_pair(stored, target, columns)
    return jnp.einsum("rk,rl->kl", left_rows, right_rows, precision=highest)


def eliminate(stored, near_matrix, interp_box):
    box_points = near_matrix.shape[0]
    skel_count = interp_box.shape[0]
    fill_blocks = [cross_sum(stored, m, box_points) for m in offsets_all()]
    matrix = near_matrix - jnp.concatenate(fill_blocks, axis=1)
    reduced_rows = matrix[skel_count:] - jnp.einsum(
        "sr,sk->rk", interp_box, matrix[:skel_count], precision=highest
    )
    centre = reduced_rows[:, 4 * box_points : 5 * box_points]
    reduced = centre[:, skel_count:] - jnp.einsum(
        "rs,st->rt", centre[:, :skel_count], interp_box, precision=highest
    )
    diag_factor = jnp.linalg.cholesky(reduced)
    return jax.scipy.linalg.solve_triangular(diag_factor, reduced_rows, lower=True)


def spread(factor_new, move_first, move_second, p):
    box_points = factor_new.shape[1] // 9

    def take_block(m):
        k = block_of(m[0], m[1])
        return factor_new[:, k * box_points : (k + 1) * box_points]

    placed = {}
    section_one = {}
    for s in (1, -1):
        listing = [vector(u, v) for u in (0, s) for v in (-1, 0, 1)]
        arrived = move_first(jnp.stack([take_block(m) for m in listing]), s)
        source = vector(-s, 0)
        section_one[s] = (source, listing, arrived)
        for n, m in enumerate(listing):
            placed[source, (m[0] + source[0], m[1] + source[1])] = arrived[n]
    for t in (1, -1):
        payload = []
        labels = []
        for m in [vector(u, v) for u in (-1, 0, 1) for v in (0, t)]:
            payload.append(take_block(m))
            labels.append(((0, 0), m))
        for s in (1, -1):
            source, listing, arrived = section_one[s]
            for n, m in enumerate(listing):
                if m[1 - p] in (0, t):
                    payload.append(arrived[n])
                    labels.append((source, m))
        arrived = move_second(jnp.stack(payload), t)
        sender_at = vector(0, -t)
        for n, (anchor, m) in enumerate(labels):
            source = (anchor[0] + sender_at[0], anchor[1] + sender_at[1])
            placed[source, (m[0] + source[0], m[1] + source[1])] = arrived[n]
    for m in offsets_all():
        placed[(0, 0), m] = take_block(m)
    return jnp.stack([placed[pair] for pair in pairs_all()])


def on_device(offsets, point_order, nugget, interp):
    row_at = lax.axis_index("row")
    col_at = lax.axis_index("col")
    row_count = lax.axis_size("row")
    col_count = lax.axis_size("col")
    box_points = offsets.shape[3]
    skel_count = interp.shape[2]
    red_count = interp.shape[3]
    corner = jnp.stack([row_at, col_at]).astype(jnp.float32)[:, None]
    points = jnp.take(offsets[0, 0] + corner, point_order[0, 0], axis=1)
    weights = jnp.take(nugget[0, 0], point_order[0, 0])
    interp_box = interp[0, 0]
    neighbour_points = extended(points[None, None], (("row", 0), ("col", 1)), 1)
    present = []
    kernel_blocks = []
    for a, b in offsets_all():
        inside = (
            (row_at + a >= 0)
            & (row_at + a < row_count)
            & (col_at + b >= 0)
            & (col_at + b < col_count)
        )
        present.append(inside.astype(jnp.float32))
        kernel_block = kernel(points, neighbour_points[a + 1, b + 1]) * present[-1]
        if (a, b) == (0, 0):
            kernel_block = kernel_block + jnp.diag(weights)
        kernel_blocks.append(kernel_block)
    near_matrix = jnp.concatenate(kernel_blocks, axis=1)

    def move_first(x, amount):
        return shifted(x, "row", amount)

    def move_second(x, amount):
        return shifted(x, "col", amount)

    leading = 0
    colour = 2 * (row_at % 2) + col_at % 2
    stored = jnp.zeros((len(pairs_all()), red_count, box_points), jnp.float32)
    for k in range(4):
        factor_new = lax.cond(
            colour == k,
            lambda s: eliminate(s, near_matrix, interp_box),
            lambda s: jnp.zeros((red_count, 9 * box_points), jnp.float32),
            stored,
        )
        stored = stored + spread(factor_new, move_first, move_second, leading)
    row_width = skel_count // row_count
    col_width = skel_count // col_count
    box_total = row_count * col_count
    weights_skel = weights[:skel_count]
    pieces = []
    for k, m in enumerate(offsets_all()):
        fill_part = cross_sum(stored, m, skel_count)
        if m == (0, 0):
            delta_block = jnp.diag(weights_skel) - fill_part
        else:
            delta_block = -fill_part
        pieces.append(delta_block * present[k])
    arrived = lax.all_to_all(
        lax.all_to_all(jnp.stack(pieces), "row", split_axis=1, concat_axis=1, tiled=True),
        "col",
        split_axis=2,
        concat_axis=2,
        tiled=True,
    )
    received = jnp.transpose(
        arrived.reshape(9, row_count, row_width, col_count, col_width), (0, 2, 1, 3, 4)
    ).reshape(9, row_width, box_total, col_width)
    box_ids = jnp.arange(box_total, dtype=jnp.int32)
    src_rows = (box_ids // col_count)[:, None]
    src_cols = (box_ids % col_count)[:, None]
    all_skeleton = lax.all_gather(points[:, :skel_count][None], ("row", "col"), axis=0, tiled=True)
    row_part = lax.dynamic_slice_in_dim(all_skeleton, row_at * row_width, row_width, 2)
    col_part = lax.dynamic_slice_in_dim(all_skeleton, col_at * col_width, col_width, 2)
    row_coords = jnp.transpose(row_part, (1, 2, 0)).reshape(2, row_width * box_total)
    col_coords = jnp.transpose(col_part, (1, 2, 0)).reshape(2, col_width * box_total)
    placed = jnp.zeros((row_width, box_total, col_width, box_total), jnp.float32)
    for n, (a, b) in enumerate(offsets_all()):
        target = (src_rows + a) * col_count + src_cols + b
        living = (
            (src_rows + a >= 0)
            & (src_rows + a < row_count)
            & (src_cols + b >= 0)
            & (src_cols + b < col_count)
        )
        hit = (target == box_ids[None, :]) & living
        placed = jnp.where(hit[None, :, None, :], received[n][:, :, :, None], placed)
    delta_tile = placed.reshape(row_width * box_total, col_width * box_total)
    root_matrix = kernel(row_coords, col_coords) + delta_tile
    rows_here = root_matrix.shape[0]
    cols_here = root_matrix.shape[1]
    global_rows = row_at * rows_here + jnp.arange(rows_here, dtype=jnp.int32)
    global_cols = col_at * cols_here + jnp.arange(cols_here, dtype=jnp.int32)
    columns_out = []
    for p in range(2):
        first_col = p * PW
        owner_col = first_col // cols_here
        local_col = first_col % cols_here
        owner_row = first_col // rows_here
        local_row = first_col % rows_here
        own_slab = root_matrix[:, local_col : local_col + PW]
        slab_rows = spread_2(own_slab, "col", owner_col)
        diag_block = spread_2(slab_rows[local_row : local_row + PW], "row", owner_row)
        diag_factor = jnp.linalg.cholesky(diag_block)
        solved = jax.scipy.linalg.solve_triangular(diag_factor, slab_rows.T, lower=True).T
        pasted = lax.dynamic_update_slice(solved, diag_factor, (first_col - row_at * rows_here, 0))
        inside = (global_rows >= first_col) & (global_rows < first_col + PW)
        panel_rows = jnp.where(
            (global_rows < first_col)[:, None], 0.0, jnp.where(inside[:, None], pasted, solved)
        )
        first_global = col_at * cols_here
        holder = first_global // rows_here
        offset_rows = first_global - holder * rows_here
        panel_cols = spread_2(
            lax.dynamic_slice_in_dim(panel_rows, offset_rows, cols_here, 0), "row", holder
        )
        root_matrix = root_matrix - jnp.einsum(
            "rk,ck->rc", panel_rows, panel_cols, precision=highest
        )
        columns_out.append((owner_col, local_col, panel_rows))
    for owner_col, local_col, panel_rows in columns_out:
        current = root_matrix[:, local_col : local_col + PW]
        root_matrix = lax.dynamic_update_slice(
            root_matrix, jnp.where(col_at == owner_col, panel_rows, current), (0, local_col)
        )
    top_rows = min(2 * PW, rows_here)
    top_block = root_matrix[:top_rows]
    zero_mask = (global_rows[:top_rows, None] < 2 * PW) & (global_cols[None, :] >= 2 * PW)
    return lax.dynamic_update_slice(root_matrix, jnp.where(zero_mask, 0.0, top_block), (0, 0))


def solution(mesh):
    in_specs = (
        P("row", "col", None, None),
        P("row", "col", None),
        P("row", "col", None),
        P("row", "col", None, None),
    )
    out_specs = P("row", "col")
    return jax.shard_map(
        on_device, mesh=mesh, in_specs=in_specs, out_specs=out_specs, check_vma=False
    )
```

profile of v0, /device:TPU:3, one launch (start us, length us, event | category | flops | bytes accessed | tf_op | source)
XLA Modules:
  0.0 1412.5 jit_solution(8953518399984541422)
XLA Ops:
  33.2 21.1 %conditional.4 = (f32[128,256]{1,0:T(8,128)}, f32[128,256]{1,0:T(8,128)}, f32[128,256]{1,0:T(8,128)}, f32[128,256]{1,0:T(8,128)}, f32[128,256]{1,0:T(8,128)}, /*...) conditional(s32[]{:T(128)} %convert_element_type.55, () %tuple.65, ...), branch_computations={%region_0.1_spmd, %region_1.6_spmd} | conditional | flops 2442133504 | bytes 22315710 | solution.py:174
  92.8 37.0 %collective-permute-start.6 = (f32[14,128,256]{2,1,0:T(8,128)}, f32[14,128,256]{2,1,0:T(8,128)}, u32[]{:S(2)}, u32[]{:S(2)}) collective-permute-start(f32[14,128,256]{2,1,0:T(8,128)} %get-tuple-element.897), channel_id=1, source_target_pairs={{0,1},{1,2},{2,3},{3,4},{4,5},{5,6},{6,7},{8,9},{9,10},{10,11},{11... | collective-permute-start | bytes 5505032 | tf_op jit(solution)/shard_map/ppermute | solution.py:30
  131.7 36.3 %collective-permute-done.6 = f32[14,128,256]{2,1,0:T(8,128)} collective-permute-done((f32[14,128,256]{2,1,0:T(8,128)}, f32[14,128,256]{2,1,0:T(8,128)}, u32[]{:S(2)}, u32[]{:S(2)}) %collective-permute-start.6) | collective-permute-done | bytes 1835040 | tf_op jit(solution)/shard_map/ppermute | solution.py:30
  184.3 60.9 %conditional.5 = (f32[1,128,256]{2,1,0:T(8,128)}, f32[1,128,256]{2,1,0:T(8,128)}, f32[1,128,256]{2,1,0:T(8,128)S(1)}, f32[1,128,256]{2,1,0:T(8,128)}, f32[1,128,...) conditional(s32[]{:T(128)} %convert_element_type.56, () %tuple.67, ...), branch_computations={%region_4.7_spmd, %region_5.8_spmd} | conditional | flops 5867831296 | bytes 54264932 | solution.py:174
  218.8 11.7 cholesky.367
  280.1 26.8 %collective-permute-done.10 = f32[14,128,256]{2,1,0:T(8,128)S(1)} collective-permute-done((f32[14,128,256]{2,1,0:T(8,128)S(1)}, f32[14,128,256]{2,1,0:T(8,128)S(1)}, u32[]{:S(2)}, u32[]{:S(2)}) %collective-permute-start.10) | collective-permute-done | bytes 1835040 | tf_op jit(solution)/shard_map/ppermute | solution.py:30
  368.7 64.4 %collective-permute-start.14 = (f32[14,128,256]{2,1,0:T(8,128)}, f32[14,128,256]{2,1,0:T(8,128)}, u32[]{:S(2)}, u32[]{:S(2)}) collective-permute-start(f32[14,128,256]{2,1,0:T(8,128)} %get-tuple-element.881), channel_id=1, source_target_pairs={{0,1},{1,2},{2,3},{3,4},{4,5},{5,6},{6,7},{8,9},{9,10},{10,11},{11... | collective-permute-start | bytes 5505032 | tf_op jit(solution)/shard_map/ppermute | solution.py:30
  436.8 67.5 %all-gather.1 = f32[32,2,128]{2,1,0:T(2,128)S(1)} all-gather(f32[1,2,128]{2,1,0:T(2,128)S(1)} %copy.97), channel_id=2, replica_groups=mesh['row'=4,'col'=8] {'row','col'}, dimensions={0}, use_global_device_ids=true | all-gather | bytes 33792 | tf_op jit(solution)/shard_map/all_gather | solution.py:206
  548.7 46.4 %collective-permute-start.16 = (f32[6,128,256]{2,1,0:T(8,128)}, f32[6,128,256]{2,1,0:T(8,128)S(1)}, u32[]{:S(2)}, u32[]{:S(2)}) collective-permute-start(f32[6,128,256]{2,1,0:T(8,128)} %get-tuple-element.952), channel_id=1, source_target_pairs={{0,8},{8,16},{16,24},{1,9},{9,17},{17,25},{2,10},{10,18},{18,26},{... | collective-permute-start | bytes 2359304 | tf_op jit(solution)/shard_map/ppermute | solution.py:30
  616.7 34.2 %collective-permute-done.18 = f32[14,128,256]{2,1,0:T(8,128)} collective-permute-done((f32[14,128,256]{2,1,0:T(8,128)}, f32[14,128,256]{2,1,0:T(8,128)}, u32[]{:S(2)}, u32[]{:S(2)}) %collective-permute-start.18) | collective-permute-done | bytes 1835040 | tf_op jit(solution)/shard_map/ppermute | solution.py:30
  677.5 24.1 %all-to-all-done = f32[9,128,128]{2,0,1:T(8,128)S(1)} async-done(((f32[9,128,128]{2,0,1:T(8,128)}), f32[9,128,128]{2,0,1:T(8,128)S(1)}, u32[]{:S(2)}, u32[]{:S(2)}) %all-to-all-start) | async-done | bytes 589856 | tf_op jit(solution)/shard_map/all_to_all | solution.py:194
  706.8 13.3 all-to-all-done.1
  742.2 58.5 %all-reduce.10.cloned.1.call-done = f32[1024,512]{0,1:T(8,128)} async-done(((f32[1024,512]{0,1:T(8,128)}), f32[1024,512]{0,1:T(8,128)}) %all-reduce.10.cloned.1.call-update) | async-done | bytes 2097168 | tf_op jit(solution)/shard_map/psum | solution.py:35
  803.3 52.5 %all-reduce.12.cloned.1.call-done = f32[512,512]{0,1:T(8,128)} async-done(((f32[512,512]{0,1:T(8,128)}), f32[512,512]{0,1:T(8,128)}) %all-reduce.12.cloned.1.call-update) | async-done | bytes 1048592 | tf_op jit(solution)/shard_map/psum | solution.py:35
  857.7 11.7 cholesky.402
  869.4 9.8 custom-call.39
  879.9 11.7 cholesky.421
  892.0 10.0 custom-call.40
  903.1 11.7 cholesky.442
  925.6 12.1 cholesky.459
  951.7 39.3 %custom-call.42 = f32[4,128,128]{1,2,0:T(8,128)S(1)} custom-call(f32[4,128,128]{2,1,0:T(8,128)S(1)} %get-tuple-element.489), custom_call_target="InvertDiagBlocksLowerTriangular" | custom-call | tf_op jit(solution)/shard_map/jit(_solve_triangular)/triangular_solve | solution.py:239
  1002.4 51.3 %all-reduce.14.cloned.1.call-done = f32[512,512]{0,1:T(8,128)} async-done(((f32[512,512]{0,1:T(8,128)}), f32[512,512]{0,1:T(8,128)}) %all-reduce.14.cloned.1.call-update) | async-done | bytes 1048592 | tf_op jit(solution)/shard_map/psum | solution.py:35
  1061.6 59.3 %all-reduce.16.cloned.1.call-done = f32[1024,512]{0,1:T(8,128)} async-done(((f32[1024,512]{0,1:T(8,128)}), f32[1024,512]{0,1:T(8,128)}) %all-reduce.16.cloned.1.call-update) | async-done | bytes 2097168 | tf_op jit(solution)/shard_map/psum | solution.py:35
  1123.5 52.5 %all-reduce.18.cloned.1.call-done = f32[512,512]{0,1:T(8,128)} async-done(((f32[512,512]{0,1:T(8,128)}), f32[512,512]{0,1:T(8,128)}) %all-reduce.18.cloned.1.call-update) | async-done | bytes 1048592 | tf_op jit(solution)/shard_map/psum | solution.py:35
  1181.1 11.7 cholesky.474
  1205.9 11.7 cholesky.493
  1218.6 10.2 custom-call.44
  1232.7 11.7 cholesky.514
  1256.0 11.9 cholesky.531
  1274.9 14.6 %while.5 = (s32[]{:T(128)}, f32[512,512]{0,1:T(8,128)}, s32[4,2]{0,1:T(2,128)S(1)}, f32[4,128,128]{2,1,0:T(8,128)}, s32[]{:T(128)}) while((s32[]{:T(128)}, f32[512,512]{0,1:T(8,128)}, s32[4,2]{0,1:T(2,128)S(1)}, f32[4,128,128]{2,1,0:T(8,128)}, s32[]{:T(128)}) %tuple.518), condition=%wide.while_cond.clone, body=%wide.while_body.clone.sunk | while | flops 2 | bytes 393829 | solution.py:239
  1289.5 40.7 %custom-call.46 = f32[4,128,128]{1,2,0:T(8,128)} custom-call(f32[4,128,128]{2,1,0:T(8,128)} %get-tuple-element.490), custom_call_target="InvertDiagBlocksLowerTriangular" | custom-call | tf_op jit(solution)/shard_map/jit(_solve_triangular)/triangular_solve | solution.py:239
  1342.9 51.3 %all-reduce.20.cloned.1.call-done = f32[512,512]{0,1:T(8,128)} async-done(((f32[512,512]{0,1:T(8,128)}), f32[512,512]{0,1:T(8,128)}) %all-reduce.20.cloned.1.call-update) | async-done | bytes 1048592 | tf_op jit(solution)/shard_map/psum | solution.py:35
  (660 shorter events, 503.7 us)
Async XLA Ops:
  11.6 5.3 collective-permute-start
  14.9 5.7 collective-permute-start.1
  16.4 11.8 copy-start.23
  20.7 7.5 collective-permute-start.2
  25.8 5.8 collective-permute-start.3
  63.3 14.1 copy-start.21
  73.2 12.2 collective-permute-start.4
  78.3 12.7 collective-permute-start.5
  92.8 75.2 %collective-permute-start.6 = (f32[14,128,256]{2,1,0:T(8,128)}, f32[14,128,256]{2,1,0:T(8,128)}, u32[]{:S(2)}, u32[]{:S(2)}) collective-permute-start(f32[14,128,256]{2,1,0:T(8,128)} %get-tuple-element.897), channel_id=1, source_target_pairs={{0,1},{1,2},{2,3},{3,4},{4,5},{5,6},{6,7},{8,9},{9,10},{10,11},{11... | collective-permute-start | bytes 5505032 | tf_op jit(solution)/shard_map/ppermute | solution.py:30
  129.8 40.9 %collective-permute-start.7 = (f32[14,128,256]{2,1,0:T(8,128)}, f32[14,128,256]{2,1,0:T(8,128)}, u32[]{:S(2)}, u32[]{:S(2)}) collective-permute-start(f32[14,128,256]{2,1,0:T(8,128)} %get-tuple-element.896), channel_id=1, source_target_pairs={{1,0},{2,1},{3,2},{4,3},{5,4},{6,5},{7,6},{9,8},{10,9},{11,10},{12... | collective-permute-start | bytes 5505032 | tf_op jit(solution)/shard_map/ppermute | solution.py:30
  254.3 10.2 collective-permute-start.8
  256.5 13.3 collective-permute-start.9
  269.9 36.9 %collective-permute-start.10 = (f32[14,128,256]{2,1,0:T(8,128)S(1)}, f32[14,128,256]{2,1,0:T(8,128)S(1)}, u32[]{:S(2)}, u32[]{:S(2)}) collective-permute-start(f32[14,128,256]{2,1,0:T(8,128)S(1)} %get-tuple-element.889), channel_id=1, source_target_pairs={{0,1},{1,2},{2,3},{3,4},{4,5},{5,6},{6,7},{8,9},{9,10},{10,11},{11... | collective-permute-start | bytes 5505032 | tf_op jit(solution)/shard_map/ppermute | solution.py:30
  272.8 36.6 %collective-permute-start.11 = (f32[14,128,256]{2,1,0:T(8,128)S(1)}, f32[14,128,256]{2,1,0:T(8,128)S(1)}, u32[]{:S(2)}, u32[]{:S(2)}) collective-permute-start(f32[14,128,256]{2,1,0:T(8,128)S(1)} %get-tuple-element.888), channel_id=1, source_target_pairs={{1,0},{2,1},{3,2},{4,3},{5,4},{6,5},{7,6},{9,8},{10,9},{11,10},{12... | collective-permute-start | bytes 5505032 | tf_op jit(solution)/shard_map/ppermute | solution.py:30
  348.3 12.0 collective-permute-start.12
  354.2 12.7 collective-permute-start.13
  360.4 76.4 %copy-start.24 = (f32[2,256]{0,1:T(8,128)S(1)}, f32[2,256]{0,1:T(8,128)}, u32[]{:S(2)}) copy-start(f32[2,256]{0,1:T(8,128)} %copy-done.23) | copy-start | bytes 6148
  368.7 135.7 %collective-permute-start.14 = (f32[14,128,256]{2,1,0:T(8,128)}, f32[14,128,256]{2,1,0:T(8,128)}, u32[]{:S(2)}, u32[]{:S(2)}) collective-permute-start(f32[14,128,256]{2,1,0:T(8,128)} %get-tuple-element.881), channel_id=1, source_target_pairs={{0,1},{1,2},{2,3},{3,4},{4,5},{5,6},{6,7},{8,9},{9,10},{10,11},{11... | collective-permute-start | bytes 5505032 | tf_op jit(solution)/shard_map/ppermute | solution.py:30
  433.1 73.6 %collective-permute-start.15 = (f32[14,128,256]{2,1,0:T(8,128)}, f32[14,128,256]{2,1,0:T(8,128)}, u32[]{:S(2)}, u32[]{:S(2)}) collective-permute-start(f32[14,128,256]{2,1,0:T(8,128)} %get-tuple-element.880), channel_id=1, source_target_pairs={{1,0},{2,1},{3,2},{4,3},{5,4},{6,5},{7,6},{9,8},{10,9},{11,10},{12... | collective-permute-start | bytes 5505032 | tf_op jit(solution)/shard_map/ppermute | solution.py:30
  548.7 47.9 %copy-start.22 = (f32[14,128,256]{2,1,0:T(8,128)}, f32[14,128,256]{2,1,0:T(8,128)S(1)}, u32[]{:S(2)}) copy-start(f32[14,128,256]{2,1,0:T(8,128)S(1)} %get-tuple-element.953) | copy-start | bytes 5505028
  548.7 55.6 %collective-permute-start.16 = (f32[6,128,256]{2,1,0:T(8,128)}, f32[6,128,256]{2,1,0:T(8,128)S(1)}, u32[]{:S(2)}, u32[]{:S(2)}) collective-permute-start(f32[6,128,256]{2,1,0:T(8,128)} %get-tuple-element.952), channel_id=1, source_target_pairs={{0,8},{8,16},{16,24},{1,9},{9,17},{17,25},{2,10},{10,18},{18,26},{... | collective-permute-start | bytes 2359304 | tf_op jit(solution)/shard_map/ppermute | solution.py:30
  597.2 12.9 collective-permute-start.17
  611.8 39.0 %collective-permute-start.18 = (f32[14,128,256]{2,1,0:T(8,128)}, f32[14,128,256]{2,1,0:T(8,128)}, u32[]{:S(2)}, u32[]{:S(2)}) collective-permute-start(f32[14,128,256]{2,1,0:T(8,128)} %get-tuple-element.873), channel_id=1, source_target_pairs={{0,1},{1,2},{2,3},{3,4},{4,5},{5,6},{6,7},{8,9},{9,10},{10,11},{11... | collective-permute-start | bytes 5505032 | tf_op jit(solution)/shard_map/ppermute | solution.py:30
  614.1 38.2 %collective-permute-start.19 = (f32[14,128,256]{2,1,0:T(8,128)}, f32[14,128,256]{2,1,0:T(8,128)S(1)}, u32[]{:S(2)}, u32[]{:S(2)}) collective-permute-start(f32[14,128,256]{2,1,0:T(8,128)} %get-tuple-element.872), channel_id=1, source_target_pairs={{1,0},{2,1},{3,2},{4,3},{5,4},{6,5},{7,6},{9,8},{10,9},{11,10},{12... | collective-permute-start | bytes 5505032 | tf_op jit(solution)/shard_map/ppermute | solution.py:30
  669.2 32.4 %all-to-all-start = ((f32[9,128,128]{2,0,1:T(8,128)}), f32[9,128,128]{2,0,1:T(8,128)S(1)}, u32[]{:S(2)}, u32[]{:S(2)}) async-start(f32[9,128,128]{2,0,1:T(8,128)} %copy.105), calls=%async_computation | async-start | bytes 2097152 | tf_op jit(solution)/shard_map/all_to_all | solution.py:194
  703.2 16.9 %all-to-all-start.1 = ((f32[9,128,128]{1,0,2:T(8,128)}), f32[9,128,128]{1,0,2:T(8,128)S(1)}, u32[]{:S(2)}, u32[]{:S(2)}) async-start(f32[9,128,128]{1,0,2:T(8,128)} %copy.106), calls=%async_computation.1 | async-start | bytes 2097152 | tf_op jit(solution)/shard_map/all_to_all | solution.py:193
  706.7 93.9 %all-reduce.10.cloned.1.call-start = ((), (), s32[]{:S(2)}) async-start(), calls=%async_computation.2 | async-start | bytes 4194304 | tf_op jit(solution)/shard_map/psum | solution.py:35
  742.1 113.6 %all-reduce.12.cloned.1.call-start = ((), (), s32[]{:S(2)}) async-start(), calls=%async_computation.3 | async-start | bytes 2097152 | tf_op jit(solution)/shard_map/psum | solution.py:35
  803.0 250.8 %all-reduce.14.cloned.1.call-start = ((), (), s32[]{:S(2)}) async-start(), calls=%async_computation.4 | async-start | bytes 2097152 | tf_op jit(solution)/shard_map/psum | solution.py:35
  1002.4 118.5 %all-reduce.16.cloned.1.call-start = ((), (), s32[]{:S(2)}) async-start(), calls=%async_computation.5 | async-start | bytes 4194304 | tf_op jit(solution)/shard_map/psum | solution.py:35
  1061.6 114.5 %all-reduce.18.cloned.1.call-start = ((), (), s32[]{:S(2)}) async-start(), calls=%async_computation.6 | async-start | bytes 2097152 | tf_op jit(solution)/shard_map/psum | solution.py:35
  1123.2 270.9 %all-reduce.20.cloned.1.call-start = ((), (), s32[]{:S(2)}) async-start(), calls=%async_computation.7 | async-start | bytes 2097152 | tf_op jit(solution)/shard_map/psum | solution.py:35
  (25 other events, 98.1 us)
Sparse Core Ops, SparseCore 0:
  742.2 58.3 all-reduce.9
  803.1 52.6 all-reduce.11
  1002.5 51.1 all-reduce.13
  1061.7 59.1 all-reduce.15
  1123.4 52.6 all-reduce.17
  1343.0 51.1 all-reduce.19
where the time goes:
time: 1420 us; the launch traced here: 1410 us
  waiting for transfers between devices  508 us (36%)
  other arithmetic  302 us (21%)
  local copies, waits for them, and re-layouts  222 us (16%)
  starting transfers between devices  199 us (14%)
  matrix products  70.1 us (5%)
  blocking collectives  67.5 us (5%)
  loops' own time  22.4 us (2%)
  between operations  21.4 us (2%)
    psum x6, waiting for transfers between devices, spread_2(): return lax.psum(kept, axis)  325 us
    ppermute x16, starting transfers between devices, shifted(): return lax.ppermute(block, axis, route)  175 us
    another operation x30, other arithmetic, on_device(): diag_factor = jnp.linalg.cholesky(diag_block)  159 us
    ppermute x16, waiting for transfers between devices, shifted(): return lax.ppermute(block, axis, route)  138 us
    unnamed x249, local copies, waits for them, and re-layouts  120 us
    another operation x7, other arithmetic, on_device(): jax.scipy.linalg.solve_triangular(diag_factor, slab_rows.T, lower=True)  82.4 us
    all_gather x1, blocking collectives, on_device(): lax.all_gather(points[:, :skel_count][None], ('row', 'col'), axis=0, tile...  67.5 us
  transfers between devices with their start and end apart: 28, of which 25 were waited for; matrix products, arithmetic and copies ran while one was open for 2% of the time, Pallas kernels for 0%

commit v1 on v0

v1 whole, which is shorter than its diff:
```python
import functools

import jax
import jax.numpy as jnp
from jax import lax
from jax.experimental import pallas as pl
from jax.experimental.pallas import tpu as pltpu
from jax.sharding import PartitionSpec as P

PW = 512
PANELS = 2
kernel_amp = 0.015625
kernel_len = 0.5
f32 = jnp.float32
bf16 = jnp.bfloat16
BLK = 128
SUB = 16
TILE = 256
VMEM = pltpu.CompilerParams(vmem_limit_bytes=56 * 1024 * 1024)
OFFS = [(a, b) for a in (-1, 0, 1) for b in (-1, 0, 1)]


def idx(a, b):
    return (a + 1) * 3 + (b + 1)


def split(x):
    hi = x.astype(bf16)
    return hi, (x - hi.astype(f32)).astype(bf16)


def dot(a, b, nt=False):
    dims = ((1,), (1,)) if nt else ((1,), (0,))
    return lax.dot_general(a, b, (dims, ((), ())), preferred_element_type=f32)


def dot_pair(a, b, nt=False):
    return dot(a[0], b[0], nt) + (dot(a[0], b[1], nt) + dot(a[1], b[0], nt))


def dot3(a, b):
    return dot_pair(split(a), split(b))


def kap(cx, cy, rx, ry, amp):
    dx = cx - rx
    dy = cy - ry
    d2 = dx * dx + dy * dy
    dist = d2 * lax.rsqrt(jnp.maximum(d2, 1e-30))
    return amp * jnp.exp(dist * (-1.0 / kernel_len))


def column_of(row):
    return jnp.broadcast_to(row, (BLK, BLK)).T


def eye(n):
    return lax.broadcasted_iota(jnp.int32, (n, n), 0) == lax.broadcasted_iota(
        jnp.int32, (n, n), 1
    )


def factor(mats):
    n = mats[0].shape[0]
    w = SUB
    unit = eye(n).astype(f32)
    cur = [jnp.concatenate([m, unit], axis=1) for m in mats]
    out = [[] for _ in mats]
    rows = lax.broadcasted_iota(jnp.int32, (w, 1), 0)
    many = range(len(mats))

    def wide(x):
        return jnp.concatenate([x, x], axis=1)

    for p in range(n // w):
        lo = p * w
        fwd = [c[:w] for c in cur]
        full = list(fwd)
        col = [[jnp.broadcast_to(f[:, lo + t : lo + t + 1], (w, n)) for t in range(w)] for f in fwd]
        for t in range(w):
            for q in many:
                r = lax.rsqrt(col[q][t][t : t + 1])
                out[q].append(fwd[q][t : t + 1] * wide(r))
                rp = r * r
                scaled = col[q][t] * rp
                fwd_new = fwd[q] - wide(scaled) * fwd[q][t : t + 1]
                g = full[q][t : t + 1] * wide(rp)
                full[q] = jnp.where(rows == t, g, full[q] - wide(col[q][t]) * g)
                for v in range(t + 1, w):
                    c = col[q][v]
                    col[q][v] = jnp.where(rows == t, c * rp, c - scaled * c[t : t + 1])
                fwd[q] = fwd_new
        rest = n - lo - w
        if rest > 0:
            for q in many:
                parts = [full[q], jnp.zeros((rest, 2 * n), f32)]
                if lo > 0:
                    parts = [jnp.zeros((lo, 2 * n), f32)] + parts
                below = cur[q][w:]
                cur[q] = below - dot3(below[:, :n], jnp.concatenate(parts, axis=0))
    return [jnp.concatenate(o, axis=0) for o in out]


class Boxes:
    def __init__(self, sides):
        self.sides = sides
        self.kept = {}

    def row(self, c, n):
        return self.sides[c[1]][c[0] + 1, BLK + n : BLK + n + 1, :]

    def once(self, key, make):
        if key not in self.kept:
            self.kept[key] = make()
        return self.kept[key]

    def interp(self, c):
        return self.once(("i", c), lambda: split(self.sides[c[1]][c[0] + 1, :BLK, :]))

    def interp_t(self, c):
        return self.once(("t", c), lambda: split(self.sides[c[1]][c[0] + 1, :BLK, :].T))

    def col(self, c, n):
        return self.once(("c", c, n), lambda: column_of(self.row(c, n)))

    def kernel(self, c, part, m, part_m):
        amp = kernel_amp * self.row(c, 6) * self.row(m, 6)
        value = kap(
            self.col(c, part),
            self.col(c, 2 + part),
            self.row(m, part_m),
            self.row(m, 2 + part_m),
            amp,
        )
        if c == m and part == part_m:
            weight = self.row(c, 4 + part) + (1.0 - self.row(c, 6))
            value = value + jnp.where(eye(BLK), weight, 0.0)
        return value

    def rows_of(self, c, wanted):
        result = {}
        wanted = list(wanted)
        for n in range(0, len(wanted), 2):
            pair = wanted[n : n + 2]
            skel = jnp.concatenate([self.kernel(c, 0, m, p) for m, p in pair], axis=1)
            red = jnp.concatenate([self.kernel(c, 1, m, p) for m, p in pair], axis=1)
            value = red - dot_pair(self.interp_t(c), split(skel))
            for k, key in enumerate(pair):
                result[key] = value[:, k * BLK : (k + 1) * BLK]
        return result


def reduced(pair, interp):
    return pair[1] - dot_pair(split(pair[0]), interp)


def subtract_fill(rows, factor_e, at, interp, keys):
    gain = split(reduced((factor_e[at, 0], factor_e[at, 1]), interp).T)
    keys = [k for k in keys if k in rows]
    for n in range(0, len(keys), 2):
        pair = keys[n : n + 2]
        value = dot_pair(gain, split(jnp.concatenate([factor_e[k] for k in pair], axis=1)))
        for k, key in enumerate(pair):
            rows[key] = rows[key] - value[:, k * BLK : (k + 1) * BLK]


def solve(rows_list, centres, interps):
    mats = [reduced((r[c, 0], r[c, 1]), i) for r, c, i in zip(rows_list, centres, interps)]
    inverses = [split(u[:, BLK:]) for u in factor(mats)]
    results = []
    for rows, centre, inv in zip(rows_list, centres, inverses):
        keys = [k for k in rows if k != (centre, 1)]
        result = {}
        for n in range(0, len(keys), 2):
            pair = keys[n : n + 2]
            value = dot_pair(inv, split(jnp.concatenate([rows[k] for k in pair], axis=1)))
            for k, key in enumerate(pair):
                result[key] = value[:, k * BLK : (k + 1) * BLK]
        results.append(result)
    return results


def zero_fill(ref, start=0):
    for n in range(start, ref.shape[0]):
        ref[n] = jnp.zeros(ref.shape[1:], f32)


OWN = (0, 0)
ALL_SKEL = [(m, 0) for m in OFFS]


def first_kernel(colour, mid, left, right, h_ref, f_ref, to_left, to_right):
    boxes = Boxes({0: mid, -1: left, 1: right})
    if colour < 2:
        zero_fill(h_ref)
        zero_fill(to_left)
        zero_fill(to_right)
    else:
        zero_fill(f_ref)
    own_keys = ALL_SKEL + [(OWN, 1)]
    if colour == 0:
        sources = []
        wanted = []
    elif colour == 1:
        sources = [(0, b) for b in (-1, 1)]
        wanted = [
            [(OWN, 0), (OWN, 1), ((-1, 0), 0), ((1, 0), 0)]
            + [((a, b), 0) for a in (-1, 0, 1)]
            + [((0, b), 1)]
            for _, b in sources
        ]
    elif colour == 2:
        sources = [(a, 0) for a in (-1, 1)]
        wanted = [
            [((0, b), p) for b in (-1, 0, 1) for p in (0, 1)]
            + [((a, b), 0) for b in (-1, 0, 1)]
            + [((a, 0), 1)]
            for a, _ in sources
        ]
        own_keys = own_keys + [((0, -1), 1), ((0, 1), 1)]
    else:
        sources = [(a, b) for a in (-1, 1) for b in (-1, 1)]
        wanted = [
            [(m, p) for m in (OWN, (a, 0), (0, b), (a, b)) for p in (0, 1)] for a, b in sources
        ]
    if sources:
        first = solve(
            [boxes.rows_of(c, k) for c, k in zip(sources, wanted)],
            sources,
            [boxes.interp(c) for c in sources],
        )
        first = dict(zip(sources, first))
    own = boxes.rows_of(OWN, own_keys)
    for e in sources:
        subtract_fill(own, first[e], OWN, boxes.interp(OWN), first[e].keys())
    if colour < 2:
        result = solve([own], [OWN], [boxes.interp(OWN)])[0]
        for m in OFFS:
            f_ref[idx(*m)] = result[m, 0]
        return
    if colour == 3:
        second_at = [(-1, 0), (1, 0)]
        rows = []
        for a, _ in second_at:
            keys = [((a, 0), 0), ((a, 0), 1), (OWN, 0), (OWN, 1)]
            keys += [((0, b), p) for b in (-1, 1) for p in (0, 1)]
            keys += [((a, b), 0) for b in (-1, 1)]
            part = boxes.rows_of((a, 0), keys)
            for b in (-1, 1):
                f = first[a, b]
                subtract_fill(part, f, (a, 0), boxes.interp((a, 0)), f.keys())
            rows.append(part)
        second = solve(rows, second_at, [boxes.interp(c) for c in second_at])
        for c, f in zip(second_at, second):
            subtract_fill(own, f, OWN, boxes.interp(OWN), f.keys())
        for b, ref in ((-1, to_left), (1, to_right)):
            total = {}
            at = (0, b)
            order = [((a, v), 0) for a in (-1, 0, 1) for v in (b, 0)] + [(at, 1), (OWN, 1)]
            for key in order:
                total[key] = jnp.zeros((BLK, BLK), f32)
            for f in second:
                subtract_fill(total, f, at, boxes.interp(at), f.keys())
            for n, key in enumerate(order):
                ref[n] = -total[key]
    for key, value in own.items():
        if key[1] == 0:
            h_ref[idx(*key[0])] = value
        else:
            h_ref[red_slot(key[0][1])] = value


def red_slot(b):
    return {0: 9, -1: 10, 1: 11}[b]


def second_kernel(h_ref, from_left, from_right, interp, f_ref, to_left, to_right):
    rows = {(m, 0): h_ref[idx(*m)] for m in OFFS}
    for b in (-1, 0, 1):
        rows[(0, b), 1] = h_ref[red_slot(b)]
    for b, ref in ((-1, from_left), (1, from_right)):
        order = [((a, v), 0) for a in (-1, 0, 1) for v in (0, b)] + [(OWN, 1), ((0, b), 1)]
        for n, key in enumerate(order):
            rows[key] = rows[key] - ref[n]
    result = solve([rows], [OWN], [split(interp[...])])[0]
    for m in OFFS:
        f_ref[idx(*m)] = result[m, 0]
    for b, ref in ((-1, to_left), (1, to_right)):
        for n, key in enumerate(
            [((a, v), 0) for a in (-1, 0, 1) for v in (0, b)] + [((0, b), 1)]
        ):
            ref[n] = result[key]


def side_blocks(values, to_left, to_right):
    for b, ref in ((-1, to_left), (1, to_right)):
        for n, m in enumerate([(a, v) for a in (-1, 0, 1) for v in (0, b)]):
            ref[n] = values[m]


def third_kernel(h_ref, from_left, from_right, interp, f_ref, to_left, to_right):
    rows = {(m, 0): h_ref[idx(*m)] for m in OFFS}
    rows[OWN, 1] = h_ref[9]
    own_interp = split(interp[...])
    for b, ref in ((-1, from_left), (1, from_right)):
        f = {}
        for n, key in enumerate(
            [((a, v), 0) for a in (-1, 0, 1) for v in (b, 0)] + [(OWN, 1)]
        ):
            f[key] = ref[n]
        subtract_fill(rows, f, OWN, own_interp, f.keys())
    result = solve([rows], [OWN], [own_interp])[0]
    values = {m: result[m, 0] for m in OFFS}
    for m in OFFS:
        f_ref[idx(*m)] = values[m]
    side_blocks(values, to_left, to_right)


def pass_kernel(old_ref, f_ref, to_left, to_right):
    values = {m: old_ref[idx(*m)] for m in OFFS}
    for m in OFFS:
        f_ref[idx(*m)] = values[m]
    side_blocks(values, to_left, to_right)


def sums_kernel(f_ref, from_left, from_right, t_ref, up_ref, down_ref):
    f = {OWN: {m: split(f_ref[idx(*m)]) for m in OFFS}}
    for b, ref in ((-1, from_left), (1, from_right)):
        f[0, b] = {
            m: split(ref[n]) for n, m in enumerate([(a, v) for a in (-1, 0, 1) for v in (b, 0)])
        }
    turned = {
        (e, a): tuple(x.T for x in split_f32(f_ref, from_left, from_right, e, a))
        for e in f
        for a in (-1, 0, 1)
    }
    for a, ref in ((-1, up_ref), (0, t_ref), (1, down_ref)):
        across = [m for m in OFFS if a == 0 or m[0] in (0, a)]
        for n, m in enumerate(across):
            total = None
            for e in f:
                if m in f[e]:
                    term = dot_pair(split(turned[e, a][0]), f[e][m])
                    total = term if total is None else total + term
            ref[n] = total


def split_f32(f_ref, from_left, from_right, e, a):
    if e == OWN:
        return (f_ref[idx(a, 0)],)
    ref = from_left if e[1] < 0 else from_right
    return (ref[2 * (a + 1) + 1],)


def assemble(pack_ref, row_ref, col_ref, out_ref, colx, coly, grid_cols):
    boxes, height, _ = pack_ref.shape
    width = out_ref.shape[1]
    per = TILE // boxes
    depth = 9 * per
    tiles = width // TILE
    for i in range(out_ref.shape[0] // BLK):
        colx[i * BLK : (i + 1) * BLK, :] = column_of(row_ref[0:1, i * BLK : (i + 1) * BLK])
        coly[i * BLK : (i + 1) * BLK, :] = column_of(row_ref[1:2, i * BLK : (i + 1) * BLK])
    r = lax.broadcasted_iota(jnp.int32, (depth, TILE), 0)
    c = lax.broadcasted_iota(jnp.int32, (depth, TILE), 1)
    n, inner = r // per, r % per
    box = c % boxes
    same = inner == c // boxes
    box_row, box_col = box // grid_cols - (n // 3 - 1), box % grid_cols - (n % 3 - 1)

    def group(g, carry):
        values = []
        for s in range(8):
            b = g * 8 + s
            hot = same & (box_row == b // grid_cols) & (box_col == b % grid_cols)
            hot = hot.astype(f32).astype(bf16)
            data = pack_ref[b]
            data = jnp.concatenate(
                [data[:, t * depth : (t + 1) * depth] for t in range(tiles)], axis=0
            )
            hi, lo = split(data)
            values.append(dot(hi, hot) + dot(lo, hot))
        for t in range(tiles):
            part = jnp.stack([v[t * height : (t + 1) * height] for v in values], axis=0)
            part = jnp.swapaxes(part, 0, 1)
            rx = col_ref[0:1, t * TILE : (t + 1) * TILE]
            ry = col_ref[1:2, t * TILE : (t + 1) * TILE]
            for k in range(height):
                at = pl.ds(pl.multiple_of(k * boxes + g * 8, 8), 8)
                cx, cy = colx[at, :], coly[at, :]
                cx = jnp.concatenate([cx, cx], axis=1)
                cy = jnp.concatenate([cy, cy], axis=1)
                out_ref[at, t * TILE : (t + 1) * TILE] = part[k] + kap(cx, cy, rx, ry, kernel_amp)
        return carry

    lax.fori_loop(0, boxes // 8, group, 0)


def lead_kernel(grid_cols, pack_ref, pts_ref, uh_ref, ul_ref, ih_ref, il_ref, mat, colx, coly, rh, rl):
    assemble(pack_ref, pts_ref, pts_ref, mat, colx, coly, grid_cols)
    size = mat.shape[0]
    count = size // BLK

    def step(p, carry):
        at = pl.ds(pl.multiple_of(p * BLK, BLK), BLK)
        inv = factor([mat[at, at]])[0][:, BLK:]
        mine = dot_pair(split(inv), split(mat[at, :]))
        mat[at, :] = mine
        hi, lo = split(mine)
        rh[...] = hi
        rl[...] = lo
        uh_ref[at, :] = hi
        ul_ref[at, :] = lo
        turned = inv.T
        half = p % 2
        th, tl = split(turned)

        @pl.when(half == 0)
        def _():
            ih_ref[at, :BLK] = th
            il_ref[at, :BLK] = tl

        @pl.when(half == 1)
        def _():
            before = pl.ds(pl.multiple_of((p - 1) * BLK, BLK), BLK)
            first = ih_ref[before, :BLK], il_ref[before, :BLK]
            between = split(mat[before, at])
            corner = -dot_pair(split(dot_pair(first, between)), (th, tl))
            ch, cl = split(corner)
            ih_ref[before, BLK:] = ch
            il_ref[before, BLK:] = cl
            ih_ref[at, :BLK] = jnp.zeros((BLK, BLK), bf16)
            il_ref[at, :BLK] = jnp.zeros((BLK, BLK), bf16)
            ih_ref[at, BLK:] = th
            il_ref[at, BLK:] = tl

        def update(j, carry):
            there = pl.ds(pl.multiple_of(j * BLK, BLK), BLK)
            left = split(mat[at, there].T)
            mat[there, :] = mat[there, :] - dot_pair(left, (rh[...], rl[...]))
            return carry

        lax.fori_loop(p + 1, count, update, 0)
        return carry

    lax.fori_loop(0, count, step, 0)


def tile_kernel(
    grid_cols,
    place,
    xy_pack,
    own_pack,
    xy_pts,
    lead_pts,
    row_pts,
    col_pts,
    uh_ref,
    ul_ref,
    ih_ref,
    il_ref,
    out_ref,
    mat,
    colx,
    coly,
    ph,
    plo,
):
    assemble(xy_pack, xy_pts, lead_pts, mat, colx, coly, grid_cols)
    total, size = mat.shape
    rows, cols = out_ref.shape
    pair = 2 * BLK
    chunk = 256

    def solve_rows(c, carry):
        at = pl.ds(pl.multiple_of(c * chunk, chunk), chunk)
        for p in range(size // pair):
            here = slice(p * pair, (p + 1) * pair)
            acc = mat[at, here]
            if p > 0:
                before = slice(0, p * pair)
                acc = acc - dot_pair(
                    (ph[at, before], plo[at, before]), (uh_ref[before, here], ul_ref[before, here])
                )
            value = dot_pair(split(acc), (ih_ref[here, :], il_ref[here, :]))
            mat[at, here] = value
            hi, lo = split(value)
            ph[at, here] = hi
            plo[at, here] = lo
        return carry

    lax.fori_loop(0, total // chunk, solve_rows, 0)
    first_row, first_col = place[0], place[1]

    @pl.when(first_col < size)
    def _():
        r = first_row + lax.broadcasted_iota(jnp.int32, (rows, cols), 0)
        c = first_col + lax.broadcasted_iota(jnp.int32, (rows, cols), 1)
        start = pl.multiple_of(first_col, BLK)
        out_ref[...] = jnp.where(r >= c, mat[:rows, pl.ds(start, cols)], 0.0)

    @pl.when(first_col >= size)
    def _():
        assemble(own_pack, row_pts, col_pts, out_ref, colx, coly, grid_cols)

        def update(c, carry):
            at = pl.ds(pl.multiple_of(c * chunk, chunk), chunk)
            value = out_ref[at, :] - dot_pair(
                (ph[at, :], plo[at, :]), (ph[rows:, :], plo[rows:, :]), nt=True
            )
            r = first_row + c * chunk + lax.broadcasted_iota(jnp.int32, (chunk, cols), 0)
            out_ref[at, :] = jnp.where(r >= size, value, 0.0)
            return carry

        lax.fori_loop(0, rows // chunk, update, 0)


def blocks(*counts):
    return [jax.ShapeDtypeStruct((n, BLK, BLK), f32) for n in counts]


def on_device(offsets, point_order, nugget, interp):
    row_at = lax.axis_index("row")
    col_at = lax.axis_index("col")
    row_count = lax.axis_size("row")
    col_count = lax.axis_size("col")
    box_total = row_count * col_count
    skel = interp.shape[2]
    box_id = row_at * col_count + col_at
    both = ("row", "col")

    corner = jnp.stack([row_at, col_at]).astype(f32)[:, None]
    table = jnp.concatenate([offsets[0, 0] + corner, nugget[0, 0][None]], axis=0)
    table = jnp.take(table, point_order[0, 0], axis=1)
    details = jnp.concatenate(
        [table.reshape(6, BLK), jnp.ones((1, BLK), f32), jnp.zeros((1, BLK), f32)], axis=0
    )
    packed = jnp.concatenate([interp[0, 0], details], axis=0)
    skeleton = jnp.concatenate([table[:2, :skel], jnp.zeros((6, skel), f32)], axis=0)
    everyone = lax.all_to_all(
        jnp.broadcast_to(skeleton[None], (box_total,) + skeleton.shape),
        both,
        split_axis=0,
        concat_axis=0,
        tiled=True,
    )

    def hop(x, axis, distance):
        count = lax.axis_size(axis)
        return lax.ppermute(
            x, axis, [(i, i + distance) for i in range(count) if 0 <= i + distance < count]
        )

    def side_hop(x, distance, row_odd, col_odd):
        pairs = [
            (i * col_count + j, i * col_count + j + distance)
            for i in range(row_count)
            for j in range(col_count)
            if i % 2 == row_odd and j % 2 == col_odd and 0 <= j + distance < col_count
        ]
        return lax.ppermute(x, both, pairs)

    mid = jnp.stack([hop(packed, "row", 1), packed, hop(packed, "row", -1)])
    left = hop(mid, "col", 1)
    right = hop(mid, "col", -1)
    colour = 2 * (row_at % 2) + col_at % 2

    def first(n):
        def run(a, b, c):
            return pl.pallas_call(
                functools.partial(first_kernel, n),
                out_shape=blocks(12, 9, 8, 8),
                compiler_params=VMEM,
                name=f"first_{n}",
            )(a, b, c)

        return run

    h_rows, f_own, pay_left, pay_right = lax.switch(
        colour, [first(n) for n in range(4)], mid, left, right
    )
    from_right = side_hop(pay_left, -1, 1, 1)
    from_left = side_hop(pay_right, 1, 1, 1)
    own_interp = interp[0, 0]
    f_own, pay_left, pay_right = lax.cond(
        colour == 2,
        lambda f, *a: tuple(
            pl.pallas_call(
                second_kernel, out_shape=blocks(9, 7, 7), compiler_params=VMEM, name="second"
            )(*a)
        ),
        lambda f, *a: (f,) + tuple(jnp.zeros((7, BLK, BLK), f32) for _ in range(2)),
        f_own,
        h_rows,
        from_left,
        from_right,
        own_interp,
    )
    from_right = side_hop(pay_left, -1, 1, 0)
    from_left = side_hop(pay_right, 1, 1, 0)
    f_own, pay_left, pay_right = lax.cond(
        colour == 3,
        lambda f, *a: tuple(
            pl.pallas_call(
                third_kernel, out_shape=blocks(9, 6, 6), compiler_params=VMEM, name="third"
            )(*a)
        ),
        lambda f, *a: tuple(
            pl.pallas_call(
                pass_kernel, out_shape=blocks(9, 6, 6), compiler_params=VMEM, name="passed"
            )(f)
        ),
        f_own,
        h_rows,
        from_left,
        from_right,
        own_interp,
    )
    from_right = hop(pay_left, "col", -1)
    from_left = hop(pay_right, "col", 1)
    total, up, down = pl.pallas_call(
        sums_kernel, out_shape=blocks(9, 6, 6), compiler_params=VMEM, name="sums"
    )(f_own, from_left, from_right)
    from_below = hop(up, "row", -1)
    from_above = hop(down, "row", 1)
    delta = -(
        total
        + jnp.concatenate([jnp.zeros((3, BLK, BLK), f32), from_below], axis=0)
        + jnp.concatenate([from_above, jnp.zeros((3, BLK, BLK), f32)], axis=0)
    )
    centre = jnp.where(jnp.eye(skel, dtype=bool), table[2, :skel][None, :], 0.0)
    delta = delta.at[4].add(centre)

    lead = PANELS * PW
    lead_per = lead // box_total
    row_per = skel // row_count
    col_per = skel // col_count
    per = TILE // box_total

    def packed_rows(x):
        n, k, l = x.shape
        x = x.reshape(n, k, l // per, per)
        return jnp.transpose(x, (1, 2, 0, 3)).reshape(k, l // per * n * per)

    def exchange(x):
        return lax.all_to_all(x, both, split_axis=0, concat_axis=0, tiled=True)

    narrow = packed_rows(delta[:, :, :lead_per])
    lead_pack = exchange(
        jnp.broadcast_to(narrow[None, :lead_per], (box_total, lead_per, narrow.shape[1]))
    )
    row_parts = narrow.reshape(row_count, 1, row_per, -1)
    col_parts = narrow.reshape(1, col_count, col_per, -1)
    xy_pack = exchange(
        jnp.concatenate(
            [
                jnp.broadcast_to(row_parts, (row_count, col_count, row_per, narrow.shape[1])),
                jnp.broadcast_to(col_parts, (row_count, col_count, col_per, narrow.shape[1])),
            ],
            axis=2,
        ).reshape(box_total, row_per + col_per, -1)
    )
    whole = packed_rows(delta).reshape(row_count, row_per, col_count, -1)
    own_pack = exchange(jnp.transpose(whole, (0, 2, 1, 3)).reshape(box_total, row_per, -1))

    points = jnp.transpose(everyone[:, :2], (1, 2, 0))

    def flat(x):
        return jnp.pad(x.reshape(2, -1), ((0, 6), (0, 0)))

    lead_pts = flat(points[:, :lead_per])
    row_pts = lax.dynamic_slice_in_dim(points, row_at * row_per, row_per, 1)
    col_pts = lax.dynamic_slice_in_dim(points, col_at * col_per, col_per, 1)
    xy_pts = flat(jnp.concatenate([row_pts, col_pts], axis=1))
    row_pts, col_pts = flat(row_pts), flat(col_pts)
    rows_here = row_per * box_total
    cols_here = col_per * box_total
    upper_hi, upper_lo, inv_hi, inv_lo = pl.pallas_call(
        functools.partial(lead_kernel, col_count),
        out_shape=[jax.ShapeDtypeStruct((lead, lead), bf16)] * 2
        + [jax.ShapeDtypeStruct((lead, 2 * BLK), bf16)] * 2,
        scratch_shapes=[
            pltpu.VMEM((lead, lead), f32),
            pltpu.VMEM((lead, BLK), f32),
            pltpu.VMEM((lead, BLK), f32),
            pltpu.VMEM((BLK, lead), bf16),
            pltpu.VMEM((BLK, lead), bf16),
        ],
        compiler_params=VMEM,
        name="lead",
    )(lead_pack, lead_pts)
    place = jnp.stack([row_at * rows_here, col_at * cols_here]).astype(jnp.int32)
    vmem = pl.BlockSpec(memory_space=pltpu.VMEM)
    both_rows = rows_here + cols_here
    return pl.pallas_call(
        functools.partial(tile_kernel, col_count),
        in_specs=[pl.BlockSpec(memory_space=pltpu.SMEM)] + [vmem] * 10,
        out_specs=vmem,
        out_shape=jax.ShapeDtypeStruct((rows_here, cols_here), f32),
        scratch_shapes=[
            pltpu.VMEM((both_rows, lead), f32),
            pltpu.VMEM((both_rows, BLK), f32),
            pltpu.VMEM((both_rows, BLK), f32),
            pltpu.VMEM((both_rows, lead), bf16),
            pltpu.VMEM((both_rows, lead), bf16),
        ],
        compiler_params=VMEM,
        name="tile",
    )(
        place,
        xy_pack,
        own_pack,
        xy_pts,
        lead_pts,
        row_pts,
        col_pts,
        upper_hi,
        upper_lo,
        inv_hi,
        inv_lo,
    )


def solution(mesh):
    in_specs = (
        P("row", "col", None, None),
        P("row", "col", None),
        P("row", "col", None),
        P("row", "col", None, None),
    )
    return jax.shard_map(
        on_device, mesh=mesh, in_specs=in_specs, out_specs=P("row", "col"), check_vma=False
    )
```

time: 1420 us -> 302 us (0.21)
  waiting for transfers between devices: 508 us -> 75.5 us
  other arithmetic: 302 us -> 7.49 us
  local copies, waits for them, and re-layouts: 222 us -> 18 us
  starting transfers between devices: 199 us -> 77.3 us
  Pallas kernels: 0 us -> 101 us
  matrix products: 70.1 us -> 0 us
  blocking collectives: 67.5 us -> 0 us
  between operations: 21.4 us -> 0.86 us
    psum x6 -> x0, waiting for transfers between devices: 325 us -> none  [spread_2(): return lax.psum(kept, axis)]
    another operation x42 -> x2, other arithmetic: 264 us -> 0.67 us  [the longest x1 0.65 us: on_device(): jnp.stack([row_at * rows_here, col_at * cols_here]).astype(jnp.int32)]
    ppermute x20 -> x12, starting transfers between devices: 187 us -> 58.1 us  [the longest x8 55.2 us: hop(): lax.ppermute(x, axis, [(i, i + distance) for i in range(count) if 0 <= i...]
    ppermute x20 -> x12, waiting for transfers between devices: 145 us -> 16.9 us  [the longest x8 16.9 us: hop(): lax.ppermute(x, axis, [(i, i + distance) for i in range(count) if 0 <= i...]
    unnamed x249 -> x15, local copies, waits for them, and re-layouts: 120 us -> 3.38 us
    pallas_call x0 -> x5, Pallas kernels: none -> 101 us  [the longest x1 52.5 us: on_device(): pl.pallas_call(functools.partial(lead_kernel, col_count), out_shape=[jax....]
    all_gather x1 -> x0, blocking collectives: 67.5 us -> none  [on_device(): lax.all_gather(points[:, :skel_count][None], ('row', 'col'), axis=0, tile...]
    another operation x114 -> x3, local copies, waits for them, and re-layouts: 52.8 us -> 2.61 us  [the longest x43 23.7 us: on_device(): jax.scipy.linalg.solve_triangular(diag_factor, slab_rows.T, lower=True)]
  transfers between devices with their start and end apart: 28 -> 16, of which waited for: 25 -> 9; matrix products, arithmetic and copies ran while one was open for 2% -> 5% of each run, Pallas kernels for 0% -> 18%
where the time goes in v1:
time: 302 us; the launch traced here: 298 us
  Pallas kernels  101 us (33%)
  starting transfers between devices  77.3 us (26%)
  waiting for transfers between devices  75.5 us (25%)
  local copies, waits for them, and re-layouts  18 us (6%)
  loops' own time  17.1 us (6%)
  other arithmetic  7.49 us (2%)
    all_to_all x3, waiting for transfers between devices, exchange(): return lax.all_to_all(x, both, split_axis=0, concat_axis=0, tiled=True)  58.6 us
    ppermute x8, starting transfers between devices, hop(): lax.ppermute(x, axis, [(i, i + distance) for i in range(count) if 0 <= i...  55.2 us
    pallas_call x1, Pallas kernels, on_device(): pl.pallas_call(functools.partial(lead_kernel, col_count), out_shape=[jax....  52.5 us
    pallas_call x1, Pallas kernels, on_device(): pl.pallas_call(functools.partial(tile_kernel, col_count), in_specs=[pl.Bl...  32.6 us
    another operation x1, loops' own time, on_device(): lax.switch(colour, [first(n) for n in range(4)], mid, left, right)  17.1 us
    ppermute x8, waiting for transfers between devices, hop(): lax.ppermute(x, axis, [(i, i + distance) for i in range(count) if 0 <= i...  16.9 us
    all_to_all x3, starting transfers between devices, exchange(): return lax.all_to_all(x, both, split_axis=0, concat_axis=0, tiled=True)  15.8 us
    pallas_call x1, Pallas kernels, run(): pl.pallas_call(functools.partial(first_kernel, n), out_shape=blocks(12, 9...  12.2 us
  transfers between devices with their start and end apart: 16, of which 9 were waited for; matrix products, arithmetic and copies ran while one was open for 5% of the time, Pallas kernels for 18%

profile of v1, /device:TPU:3, one launch (start us, length us, event | category | flops | bytes accessed | tf_op | source)
XLA Modules:
  0.0 297.6 jit_solution(8712647086177551680)
XLA Ops:
  5.0 1.3 collective-permute-start.1
  6.3 4.0 %collective-permute-start = (f32[136,128]{1,0:T(8,128)S(1)}, f32[136,128]{1,0:T(8,128)S(1)}, u32[]{:S(2)}, u32[]{:S(2)}) collective-permute-start(f32[136,128]{1,0:T(8,128)S(1)} %maximum_maximum_fusion), channel_id=1, source_target_pairs={{0,8},{8,16},{16,24},{1,9},{9,17},{17,25},{2,10},{10,18},{18,26},{... | collective-permute-start | bytes 208904 | tf_op jit(solution)/shard_map/ppermute | solution.py:550
  10.3 1.3 collective-permute-done
  11.7 3.7 %collective-permute-start.3 = (f32[3,136,128]{2,1,0:T(8,128)S(1)}, f32[3,136,128]{2,1,0:T(8,128)S(1)}, u32[]{:S(2)}, u32[]{:S(2)}) collective-permute-start(f32[3,136,128]{2,1,0:T(8,128)S(1)} %pad_maximum_fusion.1), channel_id=1, source_target_pairs={{1,0},{2,1},{3,2},{4,3},{5,4},{6,5},{7,6},{9,8},{10,9},{11,10},{12... | collective-permute-start | bytes 626696 | tf_op jit(solution)/shard_map/ppermute | solution.py:550
  15.4 3.0 %collective-permute-start.2 = (f32[3,136,128]{2,1,0:T(8,128)S(1)}, f32[3,136,128]{2,1,0:T(8,128)S(1)}, u32[]{:S(2)}, u32[]{:S(2)}) collective-permute-start(f32[3,136,128]{2,1,0:T(8,128)S(1)} %pad_maximum_fusion.1), channel_id=1, source_target_pairs={{0,1},{1,2},{2,3},{3,4},{4,5},{5,6},{6,7},{8,9},{9,10},{10,11},{11... | collective-permute-start | bytes 626696 | tf_op jit(solution)/shard_map/ppermute | solution.py:550
  18.5 1.5 collective-permute-done.3
  20.0 1.2 collective-permute-done.2
  21.2 29.2 %conditional.3 = ((f32[12,128,128]{2,1,0:T(8,128)S(1)}, f32[9,128,128]{2,1,0:T(8,128)S(1)}, f32[8,128,128]{2,1,0:T(8,128)S(1)}, f32[8,128,128]{2,1,0:T(8,128)})) conditional(s32[]{:T(128)} %clamp.3, (f32[3,136,128]{2,1,0:T(8,128)S(1)}, f32[3,136,128]{2,1,0:T(8,128)S(1)}, f32[3,136,128]{2,1,0:T(8,128)S(1)}) %tuple.48, ...), branch_computations={%region_0.1_spmd, %region_1.2_spmd, %region_2.3_spmd, %region_3.4_... | conditional | bytes 8 | solution.py:579
  21.4 12.2 %first_1.1 = (f32[12,128,128]{2,1,0:T(8,128)S(1)}, f32[9,128,128]{2,1,0:T(8,128)S(1)}, f32[8,128,128]{2,1,0:T(8,128)S(1)}, f32[8,128,128]{2,1,0:T(8,128)}) custom-call(f32[3,136,128]{2,1,0:T(8,128)S(1)} %get-tuple-element.84.mid, f32[3,136,128]{2,1,0:T(8,128)S(1)} %get-tuple-element.85.left, f32[3,136,128]{2,1,0:T(8,128)S(1)} %get-tuple-element.86.right), custom_call_target="tpu_custom_call" | custom-call | tf_op jit(solution)/shard_map/cond/branch_1_fun/first_1/pallas_call | solution.py:570
  51.8 1.6 conditional.4
  55.8 3.5 %collective-permute-start.8 = (f32[6,128,128]{2,1,0:T(8,128)}, f32[6,128,128]{2,1,0:T(8,128)S(1)}, u32[]{:S(2)}, u32[]{:S(2)}) collective-permute-start(f32[6,128,128]{2,1,0:T(8,128)} %get-tuple-element.126), channel_id=1, source_target_pairs={{0,1},{1,2},{2,3},{3,4},{4,5},{5,6},{6,7},{8,9},{9,10},{10,11},{11... | collective-permute-start | bytes 1179656 | tf_op jit(solution)/shard_map/ppermute | solution.py:550
  59.4 1.9 collective-permute-start.9
  61.3 5.6 %collective-permute-done.8.from_left = f32[6,128,128]{2,1,0:T(8,128)S(1)} collective-permute-done((f32[6,128,128]{2,1,0:T(8,128)}, f32[6,128,128]{2,1,0:T(8,128)S(1)}, u32[]{:S(2)}, u32[]{:S(2)}) %collective-permute-start.8) | collective-permute-done | bytes 393248 | tf_op jit(solution)/shard_map/ppermute | solution.py:550
  66.9 2.5 collective-permute-done.9.from_right
  70.1 3.3 %sums.1 = (f32[9,128,128]{2,1,0:T(8,128)}, f32[6,128,128]{2,1,0:T(8,128)}, f32[6,128,128]{2,1,0:T(8,128)}) custom-call(f32[9,128,128]{2,1,0:T(8,128)S(1)} %get-tuple-element.125.f_ref, f32[6,128,128]{2,1,0:T(8,128)} %copy-done.4, f32[6,128,128]{2,1,0:T(8,128)} %copy-done.5), custom_call_target="tpu_custom_call" | custom-call | tf_op jit(solution)/shard_map/sums/pallas_call | solution.py:621
  73.4 1.3 collective-permute-start.10
  74.7 36.5 %collective-permute-start.11 = (f32[6,128,128]{2,1,0:T(8,128)}, f32[6,128,128]{2,1,0:T(8,128)S(1)}, u32[]{:S(2)}, u32[]{:S(2)}) collective-permute-start(f32[6,128,128]{2,1,0:T(8,128)} %get-tuple-element.130), channel_id=1, source_target_pairs={{0,8},{8,16},{16,24},{1,9},{9,17},{17,25},{2,10},{10,18},{18,26},{... | collective-permute-start | bytes 1179656 | tf_op jit(solution)/shard_map/ppermute | solution.py:550
  112.1 3.3 %all-to-all-start.2 = ((f32[32,8,128]{2,1,0:T(8,128)}), f32[32,8,128]{2,1,0:T(8,128)}, u32[]{:S(2)}, u32[]{:S(2)}) async-start(f32[32,8,128]{2,1,0:T(8,128)} %broadcast_in_dim.80), calls=%async_computation.2 | async-start | bytes 262144 | tf_op jit(solution)/shard_map/all_to_all | solution.py:540
  115.7 3.6 %collective-permute-done.10 = f32[6,128,128]{2,1,0:T(8,128)S(1)} collective-permute-done((f32[6,128,128]{2,1,0:T(8,128)}, f32[6,128,128]{2,1,0:T(8,128)S(1)}, u32[]{:S(2)}, u32[]{:S(2)}) %collective-permute-start.10) | collective-permute-done | bytes 393248 | tf_op jit(solution)/shard_map/ppermute | solution.py:550
  119.3 1.2 collective-permute-done.11
  122.9 2.1 copy.31
  125.1 6.4 %all-to-all-start.1 = ((f32[32,32,144]{2,1,0:T(8,128)}), f32[32,32,144]{2,1,0:T(8,128)S(1)}, u32[]{:S(2)}, u32[]{:S(2)}) async-start(f32[32,32,144]{2,1,0:T(8,128)} %bitcast.53), calls=%async_computation.1 | async-start | bytes 2097152 | tf_op jit(solution)/shard_map/all_to_all | solution.py:646
  131.8 25.3 %all-to-all-done.1.own_pack = f32[32,32,144]{2,1,0:T(8,128)S(1)} async-done(((f32[32,32,144]{2,1,0:T(8,128)}), f32[32,32,144]{2,1,0:T(8,128)S(1)}, u32[]{:S(2)}, u32[]{:S(2)}) %all-to-all-start.1) | async-done | bytes 589856 | tf_op jit(solution)/shard_map/all_to_all | solution.py:646
  157.1 1.5 broadcast_in_dim.82
  158.6 4.6 %all-to-all-start.3 = ((f32[32,32,288]{2,1,0:T(8,128)}), f32[32,32,288]{2,1,0:T(8,128)S(1)}, u32[]{:S(2)}, u32[]{:S(2)}) async-start(f32[32,32,288]{2,1,0:T(8,128)} %broadcast_in_dim.82), calls=%async_computation.3 | async-start | bytes 3145728 | tf_op jit(solution)/shard_map/all_to_all | solution.py:646
  164.9 1.6 pad_maximum_fusion
  166.5 33.3 %all-to-all-done.3.pack_ref = f32[32,32,288]{2,1,0:T(8,128)S(1)} async-done(((f32[32,32,288]{2,1,0:T(8,128)}), f32[32,32,288]{2,1,0:T(8,128)S(1)}, u32[]{:S(2)}, u32[]{:S(2)}) %all-to-all-start.3) | async-done | bytes 1179680 | tf_op jit(solution)/shard_map/all_to_all | solution.py:646
  199.8 1.1 copy-done.1
  200.9 4.8 %all-to-all-start = ((f32[32,48,288]{2,1,0:T(8,128)}), f32[32,48,288]{2,1,0:T(8,128)S(1)}, u32[]{:S(2)}, u32[]{:S(2)}) async-start(f32[32,48,288]{2,1,0:T(8,128)} %bitcast.17), calls=%async_computation | async-start | bytes 4718592 | tf_op jit(solution)/shard_map/all_to_all | solution.py:646
  210.7 52.5 %lead.1 = (bf16[1024,1024]{1,0:T(8,128)(2,1)}, bf16[1024,1024]{1,0:T(8,128)(2,1)}, bf16[1024,256]{1,0:T(8,128)(2,1)}, bf16[1024,256]{1,0:T(8,128)(2,1)}) custom-call(f32[32,32,288]{2,1,0:T(8,128)} %copy-done.1, f32[8,1024]{1,0:T(8,128)} %pad.21.pts_ref.lead_pts), custom_call_target="tpu_custom_call" | custom-call | tf_op jit(solution)/shard_map/lead/pallas_call | solution.py:678
  263.2 1.4 copy-done
  264.6 32.6 %tile.1 = f32[1024,512]{1,0:T(8,128)} custom-call(s32[2]{0:T(128)} %pad_add_fusion.place, f32[32,48,288]{2,1,0:T(8,128)} %copy-done, f32[32,32,144]{2,1,0:T(8,128)} %copy-done.2, f32[8,1536]{1,0:T(8,128)} %pad.20.xy_pts, f32[8,1024]{1,0:T(8,128)} %pad.21.pts_ref.lead_pts, f32[8,1024]{1,0:T(8,128)} %pad.22.row_pts, f32[8,512]{1,0:T(8,128)} %pad.23.col_pts, ...), custom_call_target="tpu_custom_call" | custom-call | tf_op jit(solution)/shard_map/tile/pallas_call | solution.py:695
  (83 shorter events, 22.4 us)
Async XLA Ops:
  0.0 51.8 %copy-start.3 = (f32[1,1,128,128]{3,2,1,0:T(8,128)S(1)}, f32[1,1,128,128]{3,2,1,0:T(8,128)}, u32[]{:S(2)}) copy-start(f32[1,1,128,128]{3,2,1,0:T(8,128)} %param.17) | copy-start | bytes 196612
  5.0 5.3 %collective-permute-start.1 = (f32[136,128]{1,0:T(8,128)S(1)}, f32[136,128]{1,0:T(8,128)S(1)}, u32[]{:S(2)}, u32[]{:S(2)}) collective-permute-start(f32[136,128]{1,0:T(8,128)S(1)} %maximum_maximum_fusion), channel_id=1, source_target_pairs={{8,0},{16,8},{24,16},{9,1},{17,9},{25,17},{10,2},{18,10},{26,18},{... | collective-permute-start | bytes 208904 | tf_op jit(solution)/shard_map/ppermute | solution.py:550
  6.3 5.3 %collective-permute-start = (f32[136,128]{1,0:T(8,128)S(1)}, f32[136,128]{1,0:T(8,128)S(1)}, u32[]{:S(2)}, u32[]{:S(2)}) collective-permute-start(f32[136,128]{1,0:T(8,128)S(1)} %maximum_maximum_fusion), channel_id=1, source_target_pairs={{0,8},{8,16},{16,24},{1,9},{9,17},{17,25},{2,10},{10,18},{18,26},{... | collective-permute-start | bytes 208904 | tf_op jit(solution)/shard_map/ppermute | solution.py:550
  11.7 8.3 %collective-permute-start.3 = (f32[3,136,128]{2,1,0:T(8,128)S(1)}, f32[3,136,128]{2,1,0:T(8,128)S(1)}, u32[]{:S(2)}, u32[]{:S(2)}) collective-permute-start(f32[3,136,128]{2,1,0:T(8,128)S(1)} %pad_maximum_fusion.1), channel_id=1, source_target_pairs={{1,0},{2,1},{3,2},{4,3},{5,4},{6,5},{7,6},{9,8},{10,9},{11,10},{12... | collective-permute-start | bytes 626696 | tf_op jit(solution)/shard_map/ppermute | solution.py:550
  15.4 5.8 %collective-permute-start.2 = (f32[3,136,128]{2,1,0:T(8,128)S(1)}, f32[3,136,128]{2,1,0:T(8,128)S(1)}, u32[]{:S(2)}, u32[]{:S(2)}) collective-permute-start(f32[3,136,128]{2,1,0:T(8,128)S(1)} %pad_maximum_fusion.1), channel_id=1, source_target_pairs={{0,1},{1,2},{2,3},{3,4},{4,5},{5,6},{6,7},{8,9},{9,10},{10,11},{11... | collective-permute-start | bytes 626696 | tf_op jit(solution)/shard_map/ppermute | solution.py:550
  50.4 1.4 collective-permute-start.4
  51.1 0.7 collective-permute-start.5
  53.4 57.8 %copy-start.6 = (s32[1,1,256]{2,1,0:T(1,128)S(1)}, s32[1,1,256]{2,1,0:T(1,128)}, u32[]{:S(2)}) copy-start(s32[1,1,256]{2,1,0:T(1,128)} %param.15) | copy-start | bytes 3076
  53.4 1.5 collective-permute-start.6
  54.3 0.7 collective-permute-start.7
  55.8 11.0 %collective-permute-start.8 = (f32[6,128,128]{2,1,0:T(8,128)}, f32[6,128,128]{2,1,0:T(8,128)S(1)}, u32[]{:S(2)}, u32[]{:S(2)}) collective-permute-start(f32[6,128,128]{2,1,0:T(8,128)} %get-tuple-element.126), channel_id=1, source_target_pairs={{0,1},{1,2},{2,3},{3,4},{4,5},{5,6},{6,7},{8,9},{9,10},{10,11},{11... | collective-permute-start | bytes 1179656 | tf_op jit(solution)/shard_map/ppermute | solution.py:550
  59.4 10.0 %collective-permute-start.9 = (f32[6,128,128]{2,1,0:T(8,128)S(1)}, f32[6,128,128]{2,1,0:T(8,128)S(1)}, u32[]{:S(2)}, u32[]{:S(2)}) collective-permute-start(f32[6,128,128]{2,1,0:T(8,128)S(1)} %get-tuple-element.127), channel_id=1, source_target_pairs={{1,0},{2,1},{3,2},{4,3},{5,4},{6,5},{7,6},{9,8},{10,9},{11,10},{12... | collective-permute-start | bytes 1179656 | tf_op jit(solution)/shard_map/ppermute | solution.py:550
  66.9 2.5 copy-start.4
  69.4 0.7 copy-start.5
  73.4 45.8 %collective-permute-start.10 = (f32[6,128,128]{2,1,0:T(8,128)}, f32[6,128,128]{2,1,0:T(8,128)S(1)}, u32[]{:S(2)}, u32[]{:S(2)}) collective-permute-start(f32[6,128,128]{2,1,0:T(8,128)} %get-tuple-element.129), channel_id=1, source_target_pairs={{8,0},{16,8},{24,16},{9,1},{17,9},{25,17},{10,2},{18,10},{26,18},{... | collective-permute-start | bytes 1179656 | tf_op jit(solution)/shard_map/ppermute | solution.py:550
  74.7 45.7 %collective-permute-start.11 = (f32[6,128,128]{2,1,0:T(8,128)}, f32[6,128,128]{2,1,0:T(8,128)S(1)}, u32[]{:S(2)}, u32[]{:S(2)}) collective-permute-start(f32[6,128,128]{2,1,0:T(8,128)} %get-tuple-element.130), channel_id=1, source_target_pairs={{0,8},{8,16},{16,24},{1,9},{9,17},{17,25},{2,10},{10,18},{18,26},{... | collective-permute-start | bytes 1179656 | tf_op jit(solution)/shard_map/ppermute | solution.py:550
  112.1 12.9 %all-to-all-start.2 = ((f32[32,8,128]{2,1,0:T(8,128)}), f32[32,8,128]{2,1,0:T(8,128)}, u32[]{:S(2)}, u32[]{:S(2)}) async-start(f32[32,8,128]{2,1,0:T(8,128)} %broadcast_in_dim.80), calls=%async_computation.2 | async-start | bytes 262144 | tf_op jit(solution)/shard_map/all_to_all | solution.py:540
  125.1 32.0 %all-to-all-start.1 = ((f32[32,32,144]{2,1,0:T(8,128)}), f32[32,32,144]{2,1,0:T(8,128)S(1)}, u32[]{:S(2)}, u32[]{:S(2)}) async-start(f32[32,32,144]{2,1,0:T(8,128)} %bitcast.53), calls=%async_computation.1 | async-start | bytes 2097152 | tf_op jit(solution)/shard_map/all_to_all | solution.py:646
  157.1 1.5 copy-start.2
  158.6 41.2 %all-to-all-start.3 = ((f32[32,32,288]{2,1,0:T(8,128)}), f32[32,32,288]{2,1,0:T(8,128)S(1)}, u32[]{:S(2)}, u32[]{:S(2)}) async-start(f32[32,32,288]{2,1,0:T(8,128)} %broadcast_in_dim.82), calls=%async_computation.3 | async-start | bytes 3145728 | tf_op jit(solution)/shard_map/all_to_all | solution.py:646
  199.8 1.1 copy-start.1
  200.9 62.3 %all-to-all-start = ((f32[32,48,288]{2,1,0:T(8,128)}), f32[32,48,288]{2,1,0:T(8,128)S(1)}, u32[]{:S(2)}, u32[]{:S(2)}) async-start(f32[32,48,288]{2,1,0:T(8,128)} %bitcast.17), calls=%async_computation | async-start | bytes 4718592 | tf_op jit(solution)/shard_map/all_to_all | solution.py:646
  263.2 1.4 copy-start
